TPU v7x, 32 devices: a whole 2x2x4 slice. The times are simulated.
32 devices in a mesh: row: 4 (over z), col: 8 (over y, x, core).
Axes of the slice: x: 2, y: 2, z: 4, core: 2. Of those that a mesh axis runs over, the one named last changes fastest.
Arguments:
- seq_ids: int32 [1024], replicated, may hold values from 0 to 7, never falling along the last dimension, each value on 1 to 192 neighbouring positions
- attn_weights: float32 [1024, 64, 32], P(('row', 'col')), may hold values from 0.05 to 20
- values: bfloat16 [1024, 8192], P(('row', 'col')), may hold values from -6 to 6
- out_grads: bfloat16 [1024, 8192], P(('row', 'col')), may hold values from -2 to 2
- act_basis: bfloat16 [8192, 8192], P('row', 'col'), may hold values from -0.0625 to 0.0625
- grad_basis: bfloat16 [8192, 8192], P('col', 'row'), may hold values from -0.0625 to 0.0625
Outputs:
- eigenvalues: float32 [8192, 8192], P('row', 'col')
Inputs may be any that keep to these rules, and one draw needn't show every extreme that they name: `seq_ids`: ids never fall along the tokens; each of the 8 sequences is one run of 1 to 192 tokens, and one has exactly 192.
All inputs are finite; a program needn't handle non-finite values.
Results may differ from a plain program's by a relative error of at most 0.014.
Values may be sent and summed in bfloat16 or wider, within the bound.
A program may use at most 128 MiB of HBM per device.

v0:
```python
import jax
import jax.numpy as jnp
from jax import lax
from jax.sharding import PartitionSpec as P

SEQ_MEAN = 128
LONGEST = 192


def from_behind(value, axis, steps):
    count = lax.axis_size(axis)
    initial, last = (max(0, -steps), min(count, count - steps))
    return lax.ppermute(value, axis, [(source, source + steps) for source in range(initial, last)])


def shards(seq_ids, attn_weights, values, out_grads, act_basis, grad_basis):
    tok = values.shape[0]
    width = values.shape[1]
    heads = attn_weights.shape[1]
    window = attn_weights.shape[2]
    head_size = width // heads
    total_tok = seq_ids.shape[0]
    offset = lax.axis_index(("row", "col")) * tok
    previous = from_behind(values, ("row", "col"), 1)
    keys = jnp.concatenate([previous, values], axis=0).reshape(2 * tok, heads, head_size)
    query_pos = offset + jnp.arange(tok, dtype=jnp.int32)
    steps_back = jnp.arange(window, dtype=jnp.int32)
    key_pos = query_pos[:, None] - steps_back[None, :]
    key_seg = jnp.take(seq_ids, jnp.clip(key_pos, 0, total_tok - 1))
    query_seg = lax.dynamic_slice_in_dim(seq_ids, offset, tok, 0)
    valid = jnp.logical_and(key_pos >= 0, key_seg == query_seg[:, None]).astype(jnp.float32)
    masked = attn_weights * valid[:, None, :]
    probs = (masked / jnp.sum(masked, axis=2, keepdims=True)).astype(jnp.bfloat16)
    local_key = tok + jnp.arange(tok, dtype=jnp.int32)[:, None] - steps_back[None, :]
    selector = (
        local_key[:, :, None] == jnp.arange(2 * tok, dtype=jnp.int32)[None, None, :]
    ).astype(jnp.bfloat16)
    spread = jnp.einsum("phj,pjk->phk", probs, selector, preferred_element_type=jnp.float32).astype(
        jnp.bfloat16
    )
    mixed = jnp.einsum("phk,khd->phd", spread, keys, preferred_element_type=jnp.float32)
    inputs = mixed.reshape(tok, width).astype(jnp.bfloat16)
    col_tokens = lax.all_gather(inputs, "col", axis=0, tiled=True)
    act_rows = lax.all_to_all(col_tokens, "row", split_axis=1, concat_axis=0, tiled=True)
    grad_cols = lax.all_to_all(out_grads, "col", split_axis=1, concat_axis=0, tiled=True)
    block = act_rows
    act_piece = lax.psum_scatter(
        jnp.dot(block, act_basis, preferred_element_type=jnp.float32).astype(jnp.bfloat16),
        "row",
        scatter_dimension=0,
        tiled=True,
    )
    rot_inputs = lax.all_gather(act_piece, "row", axis=0, tiled=True)
    grad_all = lax.all_gather(grad_cols, "row", axis=0, tiled=True)
    block = grad_all
    grad_piece = lax.psum_scatter(
        jnp.dot(block, grad_basis, preferred_element_type=jnp.float32).astype(jnp.bfloat16),
        "col",
        scatter_dimension=0,
        tiled=True,
    )
    rot_grads = lax.all_gather(grad_piece, "col", axis=0, tiled=True)
    sequences = total_tok // SEQ_MEAN
    seq_range = jnp.arange(sequences, dtype=jnp.int32)
    starts = jnp.sum((seq_ids[None, :] < seq_range[:, None]).astype(jnp.int32), axis=1)

    def accumulate(index, running):
        first = jnp.minimum(starts[index], total_tok - LONGEST)
        grad_win = lax.dynamic_slice_in_dim(rot_grads, first, LONGEST, 0)
        act_win = lax.dynamic_slice_in_dim(rot_inputs, first, LONGEST, 0)
        seg_win = lax.dynamic_slice_in_dim(seq_ids, first, LONGEST, 0)
        grad_win = jnp.where((seg_win == index)[:, None], grad_win, jnp.zeros_like(grad_win))
        tile = lax.dot_general(
            grad_win, act_win, (((0,), (0,)), ((), ())), preferred_element_type=jnp.float32
        )
        return running + tile * tile

    start_acc = jnp.zeros((rot_grads.shape[1], rot_inputs.shape[1]), jnp.float32)
    running = lax.fori_loop(0, sequences, accumulate, start_acc)
    return running / sequences


def solution(mesh):
    return jax.shard_map(
        shards,
        mesh=mesh,
        in_specs=(
            P(),
            P(("row", "col"), None, None),
            P(("row", "col"), None),
            P(("row", "col"), None),
            P("row", "col"),
            P("col", "row"),
        ),
        out_specs=P("row", "col"),
        check_vma=False,
    )
```

profile of v0, /device:TPU:1, one launch (start us, length us, event | category | flops | bytes accessed | tf_op | source)
XLA Modules:
  0.0 428.5 jit_solution(16820139501933862641)
XLA Ops:
  6.5 4.6 %collective-permute-start = (bf16[32,8192]{1,0:T(8,128)(2,1)}, bf16[32,8192]{1,0:T(8,128)(2,1)S(1)}, u32[]{:S(2)}, u32[]{:S(2)}) collective-permute-start(bf16[32,8192]{1,0:T(8,128)(2,1)} %param.10), channel_id=1, source_target_pairs={{0,1},{1,2},{2,3},{3,4},{4,5},{5,6},{6,7},{7,8},{8,9},{9,10},{10,1... | collective-permute-start | bytes 1572872 | tf_op jit(solution)/shard_map/ppermute | solution.py:13
  11.4 0.8 dynamic_slice.31
  12.1 4.5 %gather_fusion = s32[1024]{0:T(1024)S(1)} fusion(s32[1024]{0:T(1024)S(1)} %copy-done, s32[1024]{0:T(1024)S(1)} %broadcast_clamp_fusion), kind=kCustom, calls=%fused_computation | custom fusion | bytes 12288 | tf_op jit(solution)/shard_map/jit(_take)/gather | solution.py:29
  17.1 0.9 convolution_convert_fusion.3
  18.6 0.9 copy.39
  19.6 12.9 %all_to_all.38 = bf16[32,8,1024]{2,0,1:T(8,128)(2,1)} all-to-all(bf16[32,8,1024]{2,0,1:T(8,128)(2,1)S(1)} %bitcast.40), channel_id=1, replica_groups=mesh['row'=4,'col'=8] {'col'}, dimensions={1} | all-to-all | bytes 1048576 | tf_op jit(solution)/shard_map/all_to_all | solution.py:45
  32.5 27.9 %all-gather.9.cloned.1.call-done = bf16[256,8192]{1,0:T(8,128)(2,1)} async-done(((bf16[32,8192]{1,0:T(8,128)(2,1)}), bf16[256,8192]{1,0:T(8,128)(2,1)}) %all-gather.9.cloned.1.call-update) | async-done | bytes 4194320 | tf_op jit(solution)/shard_map/all_gather | solution.py:43
  60.4 4.7 %copy.38 = bf16[32,4,8,2048]{3,2,0,1:T(8,128)(2,1)} copy(bf16[32,4,8,2048]{3,2,1,0:T(8,128)(2,1)} %bitcast.37) | data formatting | bytes 8388608 | tf_op jit(solution)/shard_map/all_to_all | solution.py:44
  65.1 4.8 %all-to-all-start.1 = ((bf16[256,4,2048]{2,0,1:T(8,128)(2,1)}), bf16[256,4,2048]{2,0,1:T(8,128)(2,1)}, u32[]{:S(2)}, u32[]{:S(2)}) async-start(bf16[256,4,2048]{2,0,1:T(8,128)(2,1)} %bitcast.36), calls=%async_computation.2 | async-start | bytes 8388608 | tf_op jit(solution)/shard_map/all_to_all | solution.py:44
  70.0 76.4 %all-gather.5.cloned.1.call-done = bf16[1024,1024]{1,0:T(8,128)(2,1)} async-done(((bf16[256,1024]{1,0:T(8,128)(2,1)}), bf16[1024,1024]{1,0:T(8,128)(2,1)}) %all-gather.5.cloned.1.call-update) | async-done | bytes 2097168 | tf_op jit(solution)/shard_map/all_gather | solution.py:54
  146.5 9.3 %convolution_convert_fusion = bf16[1024,2048]{1,0:T(8,128)(2,1)} fusion(bf16[1024,1024]{1,0:T(8,128)(2,1)} %all-gather.5.cloned.1.call-done, bf16[1024,2048]{1,0:T(8,128)(2,1)} %param.13), kind=kOutput, calls=%fused_computation.12 | convolution fusion | flops 4297064448 | bytes 10485760 | tf_op jit(solution)/shard_map/dot_general | solution.py:57
  155.9 41.2 %all-to-all-done.1 = bf16[256,4,2048]{2,0,1:T(8,128)(2,1)} async-done(((bf16[256,4,2048]{2,0,1:T(8,128)(2,1)}), bf16[256,4,2048]{2,0,1:T(8,128)(2,1)}, u32[]{:S(2)}, u32[]{:S(2)}) %all-to-all-start.1) | async-done | bytes 4194336 | tf_op jit(solution)/shard_map/all_to_all | solution.py:44
  197.1 9.3 %convolution_convert_fusion.1 = bf16[1024,1024]{1,0:T(8,128)(2,1)} fusion(bf16[1024,2048]{1,0:T(8,128)(2,1)} %bitcast.4, bf16[2048,1024]{1,0:T(8,128)(2,1)} %param.12), kind=kOutput, calls=%fused_computation.13 | convolution fusion | flops 4296015872 | bytes 10485760 | tf_op jit(solution)/shard_map/dot_general | solution.py:48
  207.1 44.4 %reduce-scatter.5.cloned.1.call-done = bf16[256,1024]{1,0:T(8,128)(2,1)} async-done(((bf16[1024,1024]{1,0:T(8,128)(2,1)}), bf16[256,1024]{1,0:T(8,128)(2,1)}) %reduce-scatter.5.cloned.1.call-update) | async-done | bytes 524304 | tf_op jit(solution)/shard_map/reduce_scatter | solution.py:47
  251.7 38.2 %all-gather.7.cloned.1.call-done = bf16[1024,2048]{1,0:T(8,128)(2,1)} async-done(((bf16[128,2048]{1,0:T(8,128)(2,1)}), bf16[1024,2048]{1,0:T(8,128)(2,1)}) %all-gather.7.cloned.1.call-update) | async-done | bytes 4194320 | tf_op jit(solution)/shard_map/all_gather | solution.py:62
  289.9 47.0 %all-gather.11.cloned.1.call-done = bf16[1024,1024]{1,0:T(8,128)(2,1)} async-done(((bf16[256,1024]{1,0:T(8,128)(2,1)}), bf16[1024,1024]{1,0:T(8,128)(2,1)}) %all-gather.11.cloned.1.call-update) | async-done | bytes 2097168 | tf_op jit(solution)/shard_map/all_gather | solution.py:53
  336.9 76.0 %while.14 = (s32[]{:T(128)}, f32[2048,1024]{1,0:T(8,128)}, s32[8]{0:T(128)S(1)}, s32[1024]{0:T(1024)S(1)}, bf16[1024,2048]{1,0:T(8,128)(2,1)}, /*index=5*/bf16[1...) while((s32[]{:T(128)}, f32[2048,1024]{1,0:T(8,128)}, s32[8]{0:T(128)S(1)}, ...), condition=%wide.region_5.6_spmd.clone, body=%wide.region_4.5_spmd.clone.sunk | while | flops 811991232 | bytes 17959736 | solution.py:79
  336.9 0.6 dynamic_slice.50
  338.1 6.1 %select_add_fusion.2 = f32[2048,1024]{1,0:T(8,128)} fusion(f32[2048,1024]{1,0:T(8,128)} %get-tuple-element.196, pred[]{:T(512)S(6)} %compare.3, bf16[1024,2048]{1,0:T(8,128)(2,1)} %get-tuple-element.209, s32[]{:T(128)S(6)} %select_n.81, pred[192]{0:T(512)(128)(4,1)S(1)} %dynamic-slice_compare_fusion.2, bf16[1024,1024]{1,0:T(8,128)(2,1)} %get-tuple-element.210), kind=kOutput, calls=%fused_computation.1.clone.1 | convolution fusion | flops 811991040 | bytes 17958592 | tf_op jit(solution)/shard_map/while/body/eval_jaxpr/dot_general | solution.py:73
  344.2 0.6 dynamic_slice.50
  345.4 8.6 %select_add_fusion.2 = f32[2048,1024]{1,0:T(8,128)} fusion(f32[2048,1024]{1,0:T(8,128)} %get-tuple-element.196, pred[]{:T(512)S(6)} %compare.3, bf16[1024,2048]{1,0:T(8,128)(2,1)} %get-tuple-element.209, s32[]{:T(128)S(6)} %select_n.81, pred[192]{0:T(512)(128)(4,1)S(1)} %dynamic-slice_compare_fusion.2, bf16[1024,1024]{1,0:T(8,128)(2,1)} %get-tuple-element.210), kind=kOutput, calls=%fused_computation.1.clone.1 | convolution fusion | flops 811991040 | bytes 17958592 | tf_op jit(solution)/shard_map/while/body/eval_jaxpr/dot_general | solution.py:73
  354.0 0.6 dynamic_slice.50
  355.2 8.6 %select_add_fusion.2 = f32[2048,1024]{1,0:T(8,128)} fusion(f32[2048,1024]{1,0:T(8,128)} %get-tuple-element.196, pred[]{:T(512)S(6)} %compare.3, bf16[1024,2048]{1,0:T(8,128)(2,1)} %get-tuple-element.209, s32[]{:T(128)S(6)} %select_n.81, pred[192]{0:T(512)(128)(4,1)S(1)} %dynamic-slice_compare_fusion.2, bf16[1024,1024]{1,0:T(8,128)(2,1)} %get-tuple-element.210), kind=kOutput, calls=%fused_computation.1.clone.1 | convolution fusion | flops 811991040 | bytes 17958592 | tf_op jit(solution)/shard_map/while/body/eval_jaxpr/dot_general | solution.py:73
  363.8 0.6 dynamic_slice.50
  365.1 8.6 %select_add_fusion.2 = f32[2048,1024]{1,0:T(8,128)} fusion(f32[2048,1024]{1,0:T(8,128)} %get-tuple-element.196, pred[]{:T(512)S(6)} %compare.3, bf16[1024,2048]{1,0:T(8,128)(2,1)} %get-tuple-element.209, s32[]{:T(128)S(6)} %select_n.81, pred[192]{0:T(512)(128)(4,1)S(1)} %dynamic-slice_compare_fusion.2, bf16[1024,1024]{1,0:T(8,128)(2,1)} %get-tuple-element.210), kind=kOutput, calls=%fused_computation.1.clone.1 | convolution fusion | flops 811991040 | bytes 17958592 | tf_op jit(solution)/shard_map/while/body/eval_jaxpr/dot_general | solution.py:73
  373.7 0.6 dynamic_slice.50
  374.9 8.6 %select_add_fusion.2 = f32[2048,1024]{1,0:T(8,128)} fusion(f32[2048,1024]{1,0:T(8,128)} %get-tuple-element.196, pred[]{:T(512)S(6)} %compare.3, bf16[1024,2048]{1,0:T(8,128)(2,1)} %get-tuple-element.209, s32[]{:T(128)S(6)} %select_n.81, pred[192]{0:T(512)(128)(4,1)S(1)} %dynamic-slice_compare_fusion.2, bf16[1024,1024]{1,0:T(8,128)(2,1)} %get-tuple-element.210), kind=kOutput, calls=%fused_computation.1.clone.1 | convolution fusion | flops 811991040 | bytes 17958592 | tf_op jit(solution)/shard_map/while/body/eval_jaxpr/dot_general | solution.py:73
  383.5 0.6 dynamic_slice.50
  384.7 8.6 %select_add_fusion.2 = f32[2048,1024]{1,0:T(8,128)} fusion(f32[2048,1024]{1,0:T(8,128)} %get-tuple-element.196, pred[]{:T(512)S(6)} %compare.3, bf16[1024,2048]{1,0:T(8,128)(2,1)} %get-tuple-element.209, s32[]{:T(128)S(6)} %select_n.81, pred[192]{0:T(512)(128)(4,1)S(1)} %dynamic-slice_compare_fusion.2, bf16[1024,1024]{1,0:T(8,128)(2,1)} %get-tuple-element.210), kind=kOutput, calls=%fused_computation.1.clone.1 | convolution fusion | flops 811991040 | bytes 17958592 | tf_op jit(solution)/shard_map/while/body/eval_jaxpr/dot_general | solution.py:73
  394.5 8.6 %select_add_fusion.2 = f32[2048,1024]{1,0:T(8,128)} fusion(f32[2048,1024]{1,0:T(8,128)} %get-tuple-element.196, pred[]{:T(512)S(6)} %compare.3, bf16[1024,2048]{1,0:T(8,128)(2,1)} %get-tuple-element.209, s32[]{:T(128)S(6)} %select_n.81, pred[192]{0:T(512)(128)(4,1)S(1)} %dynamic-slice_compare_fusion.2, bf16[1024,1024]{1,0:T(8,128)(2,1)} %get-tuple-element.210), kind=kOutput, calls=%fused_computation.1.clone.1 | convolution fusion | flops 811991040 | bytes 17958592 | tf_op jit(solution)/shard_map/while/body/eval_jaxpr/dot_general | solution.py:73
  404.3 8.6 %select_add_fusion.2 = f32[2048,1024]{1,0:T(8,128)} fusion(f32[2048,1024]{1,0:T(8,128)} %get-tuple-element.196, pred[]{:T(512)S(6)} %compare.3, bf16[1024,2048]{1,0:T(8,128)(2,1)} %get-tuple-element.209, s32[]{:T(128)S(6)} %select_n.81, pred[192]{0:T(512)(128)(4,1)S(1)} %dynamic-slice_compare_fusion.2, bf16[1024,1024]{1,0:T(8,128)(2,1)} %get-tuple-element.210), kind=kOutput, calls=%fused_computation.1.clone.1 | convolution fusion | flops 811991040 | bytes 17958592 | tf_op jit(solution)/shard_map/while/body/eval_jaxpr/dot_general | solution.py:73
  412.9 8.7 %broadcast_multiply_fusion = f32[2048,1024]{1,0:T(8,128)} fusion(f32[2048,1024]{1,0:T(8,128)} %get-tuple-element.114), kind=kLoop, calls=%fused_computation.11 | loop fusion | flops 2097152 | bytes 16777216 | tf_op jit(solution)/shard_map/div | solution.py:80
  (45 shorter events, 3.9 us)
Async XLA Ops:
  6.5 5.6 %copy-start = (s32[1024]{0:T(1024)S(1)}, s32[1024]{0:T(1024)}, u32[]{:S(2)}) copy-start(s32[1024]{0:T(1024)} %param.8) | copy-start | bytes 12292
  6.5 53.9 %all-gather.9.cloned.1.call-start = ((), (), s32[]{:S(2)}) async-start(), calls=%async_computation.7 | async-start | bytes 4718592 | tf_op jit(solution)/shard_map/all_gather | solution.py:43
  6.5 11.5 %collective-permute-start = (bf16[32,8192]{1,0:T(8,128)(2,1)}, bf16[32,8192]{1,0:T(8,128)(2,1)S(1)}, u32[]{:S(2)}, u32[]{:S(2)}) collective-permute-start(bf16[32,8192]{1,0:T(8,128)(2,1)} %param.10), channel_id=1, source_target_pairs={{0,1},{1,2},{2,3},{3,4},{4,5},{5,6},{6,7},{7,8},{8,9},{9,10},{10,1... | collective-permute-start | bytes 1572872 | tf_op jit(solution)/shard_map/ppermute | solution.py:13
  12.1 4.7 %copy-start.1 = (f32[32,64,32]{1,2,0:T(8,128)S(1)}, f32[32,64,32]{1,2,0:T(8,128)}, u32[]{:S(2)}) copy-start(f32[32,64,32]{1,2,0:T(8,128)} %param.9) | copy-start | bytes 786436
  12.1 5.9 %copy-start.3 = (bf16[32,8192]{1,0:T(8,128)(2,1)S(1)}, bf16[32,8192]{1,0:T(8,128)(2,1)}, u32[]{:S(2)}) copy-start(bf16[32,8192]{1,0:T(8,128)(2,1)} %param.10) | copy-start | bytes 1572868
  16.7 2.9 copy-start.2
  19.5 126.9 %all-gather.5.cloned.1.call-start = ((), (), s32[]{:S(2)}) async-start(), calls=%async_computation.4 | async-start | bytes 2621440 | tf_op jit(solution)/shard_map/all_gather | solution.py:54
  65.1 132.0 %all-to-all-start.1 = ((bf16[256,4,2048]{2,0,1:T(8,128)(2,1)}), bf16[256,4,2048]{2,0,1:T(8,128)(2,1)}, u32[]{:S(2)}, u32[]{:S(2)}) async-start(bf16[256,4,2048]{2,0,1:T(8,128)(2,1)} %bitcast.36), calls=%async_computation.2 | async-start | bytes 8388608 | tf_op jit(solution)/shard_map/all_to_all | solution.py:44
  70.0 136.5 %reduce-scatter.3.cloned.1.call-start = ((), (), s32[]{:S(2)}) async-start(), calls=%async_computation.5 | async-start | bytes 4718592 | tf_op jit(solution)/shard_map/reduce_scatter | solution.py:56
  155.8 95.7 %reduce-scatter.5.cloned.1.call-start = ((), (), s32[]{:S(2)}) async-start(), calls=%async_computation.8 | async-start | bytes 2621440 | tf_op jit(solution)/shard_map/reduce_scatter | solution.py:47
  206.4 83.5 %all-gather.7.cloned.1.call-start = ((), (), s32[]{:S(2)}) async-start(), calls=%async_computation.6 | async-start | bytes 4718592 | tf_op jit(solution)/shard_map/all_gather | solution.py:62
  207.0 129.9 %all-gather.11.cloned.1.call-start = ((), (), s32[]{:S(2)}) async-start(), calls=%async_computation.9 | async-start | bytes 2621440 | tf_op jit(solution)/shard_map/all_gather | solution.py:53
Sparse Core Ops, SparseCore 0:
  19.6 40.7 all-gather.8
  62.0 84.4 all-gather.4
  155.9 49.5 reduce-scatter.2
  207.8 43.6 reduce-scatter.4
  253.3 36.6 all-gather.6
  291.3 45.5 all-gather.10
where the time goes:
time: 430 us; the launch traced here: 428 us
  waiting for transfers between devices  276 us (64%)
  matrix products  86.3 us (20%)
  local copies, waits for them, and re-layouts  15.7 us (4%)
  between operations  13.6 us (3%)
  blocking collectives  12.9 us (3%)
  other arithmetic  9.92 us (2%)
  starting transfers between devices  9.69 us (2%)
  loops' own time  4.57 us (1%)
    all_gather x1, waiting for transfers between devices, shards(): grad_all = lax.all_gather(grad_cols, 'row', axis=0, tiled=True)  76.4 us
    dot_general x8, matrix products, accumulate(): lax.dot_general(grad_win, act_win, (((0,), (0,)), ((), ())), preferred_el...  66.2 us
    all_gather x1, waiting for transfers between devices, shards(): rot_inputs = lax.all_gather(act_piece, 'row', axis=0, tiled=True)  47 us
    reduce_scatter x1, waiting for transfers between devices, shards(): lax.psum_scatter(jnp.dot(block, act_basis, preferred_element_type=jnp.flo...  44.4 us
    all_to_all x1, waiting for transfers between devices, shards(): lax.all_to_all(col_tokens, 'row', split_axis=1, concat_axis=0, tiled=True)  41.2 us
    all_gather x1, waiting for transfers between devices, shards(): rot_grads = lax.all_gather(grad_piece, 'col', axis=0, tiled=True)  38.2 us
    all_gather x1, waiting for transfers between devices, shards(): col_tokens = lax.all_gather(inputs, 'col', axis=0, tiled=True)  27.9 us
    all_to_all x1, blocking collectives, shards(): lax.all_to_all(out_grads, 'col', split_axis=1, concat_axis=0, tiled=True)  12.9 us
  transfers between devices with their start and end apart: 8, of which 6 were waited for; matrix products, arithmetic and copies ran while one was open for 7% of the time, Pallas kernels for 0%

commit v1 on v0

v1 whole, which is shorter than its diff:
```python
import functools
import jax
import jax.numpy as jnp
from jax import lax
from jax.experimental import pallas as pl
from jax.experimental.pallas import tpu as pltpu
from jax.sharding import PartitionSpec as P

SEQ_MEAN = 128
LONGEST = 192
MIB = 1 << 20


def from_behind(value, axis, steps):
    count = lax.axis_size(axis)
    initial, last = (max(0, -steps), min(count, count - steps))
    return lax.ppermute(value, axis, [(source, source + steps) for source in range(initial, last)])


def fit_kernel(sequences, window, bounds_ref, grads_ref, acts_ref, out_ref):
    total_tok = grads_ref.shape[0]
    positions = lax.broadcasted_iota(jnp.int32, (window, 1), 0)

    def tile(index):
        start, end = bounds_ref[index], bounds_ref[index + 1]
        first = pl.multiple_of(jnp.minimum(start // 16 * 16, total_tok - window), 16)
        here = positions + first
        inside = jnp.logical_and(here >= start, here < end)
        grads = grads_ref[pl.ds(first, window), :]
        grads = jnp.where(inside, grads, jnp.zeros_like(grads))
        acts = acts_ref[pl.ds(first, window), :]
        product = lax.dot_general(
            grads, acts, (((0,), (0,)), ((), ())), preferred_element_type=jnp.float32
        )
        return product * product

    out_ref[...] = tile(0)

    @pl.loop(1, sequences - 1)
    def _(index):
        out_ref[...] += tile(index)

    out_ref[...] = (out_ref[...] + tile(sequences - 1)) * (1.0 / sequences)


def fit(bounds, rot_grads, rot_inputs, sequences):
    total_tok, rows = rot_grads.shape
    columns = rot_inputs.shape[1]
    height = 256
    window = (LONGEST + 15 + 127) // 128 * 128
    return pl.pallas_call(
        functools.partial(fit_kernel, sequences, window),
        grid=(rows // height,),
        out_shape=jax.ShapeDtypeStruct((rows, columns), jnp.float32),
        in_specs=[
            pl.BlockSpec(memory_space=pltpu.SMEM),
            pl.BlockSpec((total_tok, height), lambda i: (0, i)),
            pl.BlockSpec((total_tok, columns), lambda i: (0, 0)),
        ],
        out_specs=pl.BlockSpec((height, columns), lambda i: (i, 0)),
        compiler_params=pltpu.CompilerParams(vmem_limit_bytes=32 * MIB),
        cost_estimate=pl.CostEstimate(
            flops=2 * rows * columns * window * sequences,
            bytes_accessed=4 * rows * columns + 2 * total_tok * (rows + columns),
            transcendentals=0,
        ),
    )(bounds, rot_grads, rot_inputs)


def attention(seq_ids, attn_weights, values):
    tok = values.shape[0]
    width = values.shape[1]
    heads = attn_weights.shape[1]
    window = attn_weights.shape[2]
    head_size = width // heads
    offset = lax.axis_index(("row", "col")) * tok
    previous = from_behind(values, ("row", "col"), 1)
    keys = jnp.concatenate([previous, values], axis=0).reshape(2 * tok, heads, head_size)
    query_pos = offset + jnp.arange(tok, dtype=jnp.int32)
    steps_back = jnp.arange(window, dtype=jnp.int32)
    query_seg = lax.dynamic_slice_in_dim(seq_ids, offset, tok, 0)
    run_start = jnp.sum((seq_ids[None, :] < query_seg[:, None]).astype(jnp.int32), axis=1)
    valid = (steps_back[None, :] <= (query_pos - run_start)[:, None]).astype(jnp.float32)
    masked = attn_weights * valid[:, None, :]
    probs = (masked / jnp.sum(masked, axis=2, keepdims=True)).astype(jnp.bfloat16)
    local_key = tok + jnp.arange(tok, dtype=jnp.int32)[:, None] - steps_back[None, :]
    selector = (
        local_key[:, :, None] == jnp.arange(2 * tok, dtype=jnp.int32)[None, None, :]
    ).astype(jnp.bfloat16)
    spread = jnp.einsum("phj,pjk->phk", probs, selector, preferred_element_type=jnp.float32).astype(
        jnp.bfloat16
    )
    mixed = jnp.einsum("phk,khd->phd", spread, keys, preferred_element_type=jnp.float32)
    return mixed.reshape(tok, width).astype(jnp.bfloat16)


MESH = pl.DeviceIdType.MESH


def merged(first, second):
    steps = [((i + 0.5) / len(first), 0, s) for i, s in enumerate(first)]
    steps += [((i + 0.5) / len(second), 1, s) for i, s in enumerate(second)]
    return [s for _, _, s in sorted(steps, key=lambda entry: entry[:2])]


def rotate_kernel(
    rows, cols, inputs_ref, grads_ref, act_hbm, grad_hbm, rot_grads_ref, rot_inputs_ref,
    grad_all, act_all, act_basis, grad_basis, part, pair, ring, rot_grads, act_part, down, up,
    local_sem, out_sem, a1_send, a1_recv, g1_send, g1_recv, a2_send, a2_recv, af_send, af_recv,
    g2_down, g2_up, g2_recv, pair_send, pair_recv, ring_send, ring_recv, ag_send, ag_recv,
    agf_send, agf_recv, down_send, down_recv, up_send, up_recv,
):
    chips = cols // 2
    tok = inputs_ref.shape[0]
    act_depth, act_width = act_basis.shape
    grad_depth, grad_width = grad_basis.shape
    r, c = lax.axis_index("row"), lax.axis_index("col")
    chip, core = c // 2, c % 2
    partner = (r, 2 * chip + 1 - core)
    not_last, not_first = r < rows - 1, r > 0
    pending = []

    def remote(src, dst, send, recv, device):
        return pltpu.make_async_remote_copy(
            src_ref=src, dst_ref=dst, send_sem=send, recv_sem=recv, device_id=device,
            device_id_type=MESH,
        )

    def send(copy, condition=None):
        pending.append((copy, condition))
        if condition is None:
            copy.start()
        else:
            pl.when(condition)(copy.start)

    def arrived(dst, recv, condition=None):
        copy = remote(dst, dst, recv, recv, partner)
        if condition is None:
            copy.wait_recv()
        else:
            pl.when(condition)(copy.wait_recv)

    load_grad = pltpu.make_async_copy(grad_hbm, grad_basis, local_sem.at[0])
    load_act = pltpu.make_async_copy(act_hbm, act_basis, local_sem.at[1])
    load_grad.start()
    load_act.start()

    other_rows = [(r + d) % rows for d in range(1, rows)]
    other_cols = [(c + d) % cols for d in range(1, cols)]
    other_chips = [(chip + d) % chips for d in range(1, chips)]
    barrier = pltpu.get_barrier_semaphore()
    for other in other_rows:
        pl.semaphore_signal(barrier, inc=1, device_id=(other, c), device_id_type=MESH)
    for other in other_cols:
        pl.semaphore_signal(barrier, inc=1, device_id=(r, other), device_id_type=MESH)
    pl.semaphore_wait(barrier, rows + cols - 2)

    def act_columns(row):
        return inputs_ref.at[:, pl.ds(pl.multiple_of(row * act_depth, act_depth), act_depth)]

    def grad_columns(col):
        return grads_ref.at[:, pl.ds(pl.multiple_of(col * grad_depth, grad_depth), grad_depth)]

    for other in other_rows:
        send(remote(act_columns(other), act_all.at[chip, core, r], a1_send.at[other],
                    a1_recv.at[r], (other, c)))
    for other in other_cols:
        send(remote(grad_columns(other), grad_all.at[r, chip, core], g1_send.at[other],
                    g1_recv.at[c], (r, other)))
    act_all[chip, core, r] = act_columns(r)[...]
    grad_all[r, chip, core] = grad_columns(c)[...]

    for other in other_rows:
        arrived(act_all.at[chip, core, other], a1_recv.at[other])
    for other in other_chips:
        send(remote(act_all.at[chip, core], act_all.at[chip, core], a2_send.at[other],
                    a2_recv.at[chip], (r, 2 * other + core)))
    send(remote(act_all.at[chip, core], act_all.at[chip, core], af_send.at[chip],
                af_recv.at[chip], partner))
    for other in other_cols:
        arrived(grad_all.at[r, other // 2, other % 2], g1_recv.at[other])

    order = [sorted(range(rows), key=lambda b: (abs(b - row), b)) for row in range(rows)]
    blocks = []
    for slot in range(rows):
        block = 0
        for row in range(rows):
            block = block + jnp.where(r == row, order[row][slot], 0)
        blocks.append(block)

    def grad_rotate(slot):
        block = blocks[slot]
        if slot > 0:
            arrived(grad_all.at[block], g2_recv.at[block])
        send(remote(grad_all.at[block], grad_all.at[block], g2_down.at[slot], g2_recv.at[block],
                    (jnp.minimum(r + 1, rows - 1), c)),
             jnp.logical_and(block <= r, not_last))
        send(remote(grad_all.at[block], grad_all.at[block], g2_up.at[slot], g2_recv.at[block],
                    (jnp.maximum(r - 1, 0), c)),
             jnp.logical_and(block >= r, not_first))
        if slot == 0:
            load_grad.wait()
        width = min(512, grad_width)

        @pl.loop(0, grad_width // width)
        def _(j):
            at = pl.ds(pl.multiple_of(j * width, width), width)
            term = jnp.dot(
                grad_all[block].reshape(cols * tok, grad_depth), grad_basis[:, at],
                preferred_element_type=jnp.float32,
            )
            part[block, :, :, :, at] = term.astype(jnp.bfloat16).reshape(chips, 2, tok, width)

        send(remote(part.at[block, :, 1 - core], pair.at[block], pair_send.at[slot],
                    pair_recv.at[block], partner))

    def grad_pair(slot):
        block = blocks[slot]
        arrived(pair.at[block], pair_recv.at[block])

        @pl.loop(0, chips)
        def _(k):
            total = part[block, k, core].astype(jnp.float32) + pair[block, k].astype(jnp.float32)
            part[block, k, core] = total.astype(jnp.bfloat16)

        for other in other_chips:
            send(remote(part.at[block, other, core], ring.at[block, chip],
                        ring_send.at[slot, other], ring_recv.at[block, chip],
                        (r, 2 * other + core)))

    def grad_sum(slot):
        block = blocks[slot]
        for other in other_chips:
            arrived(ring.at[block, other], ring_recv.at[block, other])
        width = min(512, grad_width)

        @pl.loop(0, grad_width // width)
        def _(j):
            at = pl.ds(pl.multiple_of(j * width, width), width)
            total = part[block, chip, core, :, at].astype(jnp.float32)
            for other in other_chips:
                total = total + ring[block, other, :, at].astype(jnp.float32)
            rot_grads[block, chip, core, :, at] = total.astype(jnp.bfloat16)

        for other in other_chips:
            send(remote(rot_grads.at[block, chip, core], rot_grads.at[block, chip, core],
                        ag_send.at[slot, other], ag_recv.at[block, chip],
                        (r, 2 * other + core)))

    def grad_share(slot):
        block = blocks[slot]
        for other in other_chips:
            arrived(rot_grads.at[block, other, core], ag_recv.at[block, other])
        send(remote(rot_grads.at[block, :, core], rot_grads.at[block, :, core],
                    agf_send.at[slot], agf_recv.at[block], partner))

    def grad_tick(tick):
        if tick < rows:
            grad_rotate(tick)
        if 0 <= tick - 1 < rows:
            grad_pair(tick - 1)
        if 0 <= tick - 2 < rows:
            grad_sum(tick - 2)
        if 0 <= tick - 3 < rows:
            grad_share(tick - 3)

    def act_rotate(step):
        k = (chip + step) % chips
        if step > 0:
            arrived(act_all.at[k, core], a2_recv.at[k])
            send(remote(act_all.at[k, core], act_all.at[k, core], af_send.at[k], af_recv.at[k],
                        partner))
        arrived(act_all.at[k, 1 - core], af_recv.at[k])
        if step == 0:
            load_act.wait()
        width = min(512, act_width)

        @pl.loop(0, act_width // width)
        def _(j):
            at = pl.ds(pl.multiple_of(j * width, width), width)
            term = jnp.dot(
                act_all[k].reshape(2 * rows * tok, act_depth), act_basis[:, at],
                preferred_element_type=jnp.float32,
            )
            act_part[k, :, :, :, at] = term.astype(jnp.bfloat16).reshape(2, rows, tok, width)

        @pl.when(r == 0)
        def _():
            down[k] = act_part[k]

        @pl.when(r == rows - 1)
        def _():
            up[k] = act_part[k]

        for half in range(2):
            send_down(k, half, r == 0)
            send_up(k, half, r == rows - 1)

    def send_down(k, half, condition):
        copy = remote(down.at[k, half], down.at[k, half], down_send.at[k, half],
                      down_recv.at[k, half], (jnp.minimum(r + 1, rows - 1), c))
        send(copy, condition)

    def send_up(k, half, condition):
        copy = remote(up.at[k, half], up.at[k, half], up_send.at[k, half],
                      up_recv.at[k, half], (jnp.maximum(r - 1, 0), c))
        send(copy, condition)

    stores = []

    def act_chain(step):
        k = (chip + step) % chips
        for half in range(2):
            @pl.when(not_first)
            def _():
                remote(down.at[k, half], down.at[k, half], down_send.at[k, half],
                       down_recv.at[k, half], partner).wait_recv()

                @pl.loop(0, rows)
                def _(q):
                    total = down[k, half, q].astype(jnp.float32)
                    total = total + act_part[k, half, q].astype(jnp.float32)
                    down[k, half, q] = total.astype(jnp.bfloat16)

            send_down(k, half, jnp.logical_and(not_first, not_last))

            @pl.when(not_last)
            def _():
                remote(up.at[k, half], up.at[k, half], up_send.at[k, half],
                       up_recv.at[k, half], partner).wait_recv()

                @pl.loop(0, rows)
                def _(q):
                    above = up[k, half, q].astype(jnp.float32)
                    own = act_part[k, half, q].astype(jnp.float32)
                    below = down[k, half, q].astype(jnp.float32)
                    up[k, half, q] = (above + own).astype(jnp.bfloat16)
                    act_part[k, half, q] = (above + below).astype(jnp.bfloat16)

            @pl.when(r == rows - 1)
            def _():
                act_part[k, half] = down[k, half]

            send_up(k, half, jnp.logical_and(not_first, not_last))
            store = pltpu.make_async_copy(
                act_part.at[k, half], rot_inputs_ref.at[:, k, half], out_sem.at[rows + 2 * step + half]
            )
            store.start()
            stores.append(store)

    ticks = [functools.partial(grad_tick, t) for t in range(rows + 3)]
    rotates = [functools.partial(act_rotate, s) for s in range(chips)]
    chains = [functools.partial(act_chain, s) for s in range(chips)]
    for step in merged(ticks[: rows - 1], rotates) + merged(chains, ticks[rows - 1 :]):
        step()
    for slot in range(rows):
        block = blocks[slot]
        arrived(rot_grads.at[block, :, 1 - core], agf_recv.at[block])
        store = pltpu.make_async_copy(rot_grads.at[block], rot_grads_ref.at[block], out_sem.at[slot])
        store.start()
        stores.append(store)
    for copy, condition in pending:
        if condition is None:
            copy.wait_send()
        else:
            pl.when(condition)(copy.wait_send)
    for store in stores:
        store.wait()


def rotate(inputs, out_grads, act_basis, grad_basis):
    rows, cols = lax.axis_size("row"), lax.axis_size("col")
    chips = cols // 2
    tok = inputs.shape[0]
    total_tok = rows * cols * tok
    act_depth, act_width = act_basis.shape
    grad_depth, grad_width = grad_basis.shape
    bf16 = jnp.bfloat16
    vmem, dma = pltpu.VMEM, pltpu.SemaphoreType.DMA
    rot_grads, rot_inputs = pl.pallas_call(
        functools.partial(rotate_kernel, rows, cols),
        out_shape=(
            jax.ShapeDtypeStruct((rows, chips, 2, tok, grad_width), bf16),
            jax.ShapeDtypeStruct((rows, chips, 2, tok, act_width), bf16),
        ),
        in_specs=[
            pl.BlockSpec(memory_space=pltpu.VMEM),
            pl.BlockSpec(memory_space=pltpu.VMEM),
            pl.BlockSpec(memory_space=pl.ANY),
            pl.BlockSpec(memory_space=pl.ANY),
        ],
        out_specs=(pl.BlockSpec(memory_space=pl.ANY), pl.BlockSpec(memory_space=pl.ANY)),
        scratch_shapes=[
            vmem((rows, chips, 2, tok, grad_depth), bf16),
            vmem((chips, 2, rows, tok, act_depth), bf16),
            vmem(act_basis.shape, bf16),
            vmem(grad_basis.shape, bf16),
            vmem((rows, chips, 2, tok, grad_width), bf16),
            vmem((rows, chips, tok, grad_width), bf16),
            vmem((rows, chips, tok, grad_width), bf16),
            vmem((rows, chips, 2, tok, grad_width), bf16),
            vmem((chips, 2, rows, tok, act_width), bf16),
            vmem((chips, 2, rows, tok, act_width), bf16),
            vmem((chips, 2, rows, tok, act_width), bf16),
            dma((2,)), dma((rows + cols,)),
            dma((rows,)), dma((rows,)), dma((cols,)), dma((cols,)),
            dma((chips,)), dma((chips,)), dma((chips,)), dma((chips,)),
            dma((rows,)), dma((rows,)), dma((rows,)),
            dma((rows,)), dma((rows,)),
            dma((rows, chips)), dma((rows, chips)), dma((rows, chips)), dma((rows, chips)),
            dma((rows,)), dma((rows,)),
            dma((chips, 2)), dma((chips, 2)), dma((chips, 2)), dma((chips, 2)),
        ],
        compiler_params=pltpu.CompilerParams(
            collective_id=0, has_side_effects=True, vmem_limit_bytes=58 * MIB
        ),
        cost_estimate=pl.CostEstimate(
            flops=2 * total_tok * (act_depth * act_width + grad_depth * grad_width),
            bytes_accessed=4 * (act_depth * act_width + grad_depth * grad_width),
            transcendentals=0,
        ),
    )(inputs, out_grads, act_basis, grad_basis)
    return rot_grads.reshape(total_tok, grad_width), rot_inputs.reshape(total_tok, act_width)


def shards(seq_ids, attn_weights, values, out_grads, act_basis, grad_basis):
    total_tok = seq_ids.shape[0]
    sequences = total_tok // SEQ_MEAN
    inputs = attention(seq_ids, attn_weights, values)
    rot_grads, rot_inputs = rotate(inputs, out_grads, act_basis, grad_basis)
    seq_range = jnp.arange(sequences + 1, dtype=jnp.int32)
    bounds = jnp.sum((seq_ids[None, :] < seq_range[:, None]).astype(jnp.int32), axis=1)
    return fit(bounds, rot_grads, rot_inputs, sequences)

def solution(mesh):
    return jax.shard_map(
        shards,
        mesh=mesh,
        in_specs=(
            P(),
            P(("row", "col"), None, None),
            P(("row", "col"), None),
            P(("row", "col"), None),
            P("row", "col"),
            P("col", "row"),
        ),
        out_specs=P("row", "col"),
        check_vma=False,
    )
```

time: 430 us -> 214 us (0.50)
  waiting for transfers between devices: 276 us -> 0.63 us
  Pallas kernels: 0 us -> 197 us
  matrix products: 86.3 us -> 3.48 us
  between operations: 13.6 us -> 0.06 us
  blocking collectives: 12.9 us -> 0 us
  local copies, waits for them, and re-layouts: 15.7 us -> 5.43 us
  other arithmetic: 9.92 us -> 3.11 us
  starting transfers between devices: 9.69 us -> 4.5 us
  loops' own time: 4.57 us -> 0 us
    pallas_call x0 -> x2, Pallas kernels: none -> 197 us  [the longest x1 172 us: rotate(): pl.pallas_call(functools.partial(rotate_kernel, rows, cols), out_shape=(j...]
    all_gather x4 -> x0, waiting for transfers between devices: 189 us -> none  [the longest x1 76.4 us: shards(): grad_all = lax.all_gather(grad_cols, 'row', axis=0, tiled=True)]
    dot_general x12 -> x2, matrix products: 86.3 us -> 3.48 us  [the longest x1 1.9 us: attention(): jnp.einsum('phj,pjk->phk', probs, selector, preferred_element_type=jnp.fl...]
    reduce_scatter x2 -> x0, waiting for transfers between devices: 44.5 us -> none  [the longest x1 44.4 us: shards(): lax.psum_scatter(jnp.dot(block, act_basis, preferred_element_type=jnp.flo...]
    all_to_all x1 -> x0, waiting for transfers between devices: 41.2 us -> none  [shards(): lax.all_to_all(col_tokens, 'row', split_axis=1, concat_axis=0, tiled=True)]
    all_to_all x1 -> x0, blocking collectives: 12.9 us -> none  [shards(): lax.all_to_all(out_grads, 'col', split_axis=1, concat_axis=0, tiled=True)]
    div x1 -> x0, other arithmetic: 8.7 us -> none  [shards(): return running / sequences]
    all_to_all x1 -> x0, starting transfers between devices: 4.85 us -> none  [shards(): lax.all_to_all(col_tokens, 'row', split_axis=1, concat_axis=0, tiled=True)]
  transfers between devices with their start and end apart: 8 -> 1, of which waited for: 6 -> 1; matrix products, arithmetic and copies ran while one was open for 7% -> 3% of each run, Pallas kernels for 0% -> 0%
where the time goes in v1:
time: 214 us
  Pallas kernels  197 us (92%)
  local copies, waits for them, and re-layouts  5.43 us (3%)
  starting transfers between devices  4.5 us (2%)
  matrix products  3.48 us (2%)
  other arithmetic  3.11 us (1%)
    pallas_call x1, Pallas kernels, rotate(): pl.pallas_call(functools.partial(rotate_kernel, rows, cols), out_shape=(j...  172 us
    pallas_call x1, Pallas kernels, fit(): pl.pallas_call(functools.partial(fit_kernel, sequences, window), grid=(ro...  24.8 us
    ppermute x1, starting transfers between devices, from_behind(): lax.ppermute(value, axis, [(source, source + steps) for source in range(i...  4.5 us
  transfers between devices with their start and end apart: 1, of which 1 were waited for; matrix products, arithmetic and copies ran while one was open for 3% of the time, Pallas kernels for 0%

profile of v1, /device:TPU:1, one launch (start us, length us, event | category | flops | bytes accessed | tf_op | source)
XLA Modules:
  0.0 213.8 jit_solution(2681394832413970686)
XLA Ops:
  0.0 4.5 %collective-permute-start = (bf16[32,8192]{1,0:T(8,128)(2,1)}, bf16[32,8192]{1,0:T(8,128)(2,1)S(1)}, u32[]{:S(2)}, u32[]{:S(2)}) collective-permute-start(bf16[32,8192]{1,0:T(8,128)(2,1)} %param.8), channel_id=1, source_target_pairs={{0,1},{1,2},{2,3},{3,4},{4,5},{5,6},{6,7},{7,8},{8,9},{9,10},{10,1... | collective-permute-start | bytes 1572872 | tf_op jit(solution)/shard_map/ppermute | solution.py:17
  4.5 0.8 convert_reduce_fusion.1.bounds_ref
  5.3 0.8 dynamic_slice.3
  6.1 0.9 convert_reduce_fusion
  7.0 0.1 fusion.7
  7.0 1.3 multiply_reduce_fusion
  8.3 0.1 iota_subtract_fusion
  8.4 1.9 convolution_convert_fusion.1
  10.3 0.6 collective-permute-done
  10.9 1.6 fusion
  12.5 0.9 copy.22
  13.4 171.8 %shard_map.64 = (bf16[4,4,2,32,2048]{4,3,2,1,0:T(8,128)(2,1)}, bf16[4,4,2,32,1024]{4,3,2,1,0:T(8,128)(2,1)}) custom-call(bf16[32,8192]{1,0:T(8,128)(2,1)} %bitcast.17, bf16[32,8192]{1,0:T(8,128)(2,1)} %grads_ref.1, bf16[2048,1024]{1,0:T(8,128)(2,1)} %act_hbm.1, bf16[1024,2048]{1,0:T(8,128)(2,1)} %grad_hbm.1), custom_call_target="tpu_custom_call" | custom-call | flops 8589934592 | bytes 16777216 | tf_op jit(solution)/shard_map/pallas_call | solution.py:380
  185.3 0.0 copy-start
  185.3 2.2 %copy-done = bf16[4,4,2,32,2048]{4,3,2,1,0:T(8,128)(2,1)S(1)} copy-done((bf16[4,4,2,32,2048]{4,3,2,1,0:T(8,128)(2,1)S(1)}, bf16[4,4,2,32,2048]{4,3,2,1,0:T(8,128)(2,1)}, u32[]{:S(2)}) %copy-start) | copy-done | bytes 4194328
  187.4 0.0 copy-start.1
  187.4 1.6 copy-done.1
  189.0 24.8 %shard_map.65 = f32[2048,1024]{1,0:T(8,128)} custom-call(s32[9]{0:T(128)S(1)} %convert_reduce_fusion.1.bounds_ref, bf16[1024,2048]{1,0:T(8,128)(2,1)S(1)} %bitcast.15, bf16[1024,1024]{1,0:T(8,128)(2,1)S(1)} %bitcast.16), custom_call_target="tpu_custom_call" | custom-call | flops 8589934592 | bytes 14680064 | tf_op jit(solution)/shard_map/pallas_call | solution.py:51
  (2 shorter events, 0.0 us)
Async XLA Ops:
  0.0 10.9 %collective-permute-start = (bf16[32,8192]{1,0:T(8,128)(2,1)}, bf16[32,8192]{1,0:T(8,128)(2,1)S(1)}, u32[]{:S(2)}, u32[]{:S(2)}) collective-permute-start(bf16[32,8192]{1,0:T(8,128)(2,1)} %param.8), channel_id=1, source_target_pairs={{0,1},{1,2},{2,3},{3,4},{4,5},{5,6},{6,7},{7,8},{8,9},{9,10},{10,1... | collective-permute-start | bytes 1572872 | tf_op jit(solution)/shard_map/ppermute | solution.py:17
  185.3 2.2 %copy-start = (bf16[4,4,2,32,2048]{4,3,2,1,0:T(8,128)(2,1)S(1)}, bf16[4,4,2,32,2048]{4,3,2,1,0:T(8,128)(2,1)}, u32[]{:S(2)}) copy-start(bf16[4,4,2,32,2048]{4,3,2,1,0:T(8,128)(2,1)} %get-tuple-element.7) | copy-start | bytes 12582916
  187.4 1.6 copy-start.1

commit v2 on v1

--- a/solution.py
+++ b/solution.py
@@ -34,13 +34,21 @@
         )
         return product * product
 
-    out_ref[...] = tile(0)
-
-    @pl.loop(1, sequences - 1)
+    group = 4
+
+    def squares(index):
+        total = tile(index)
+        for step in range(1, group):
+            total = total + tile(index + step)
+        return total
+
+    out_ref[...] = squares(0)
+
+    @pl.loop(1, sequences // group - 1)
     def _(index):
-        out_ref[...] += tile(index)
-
-    out_ref[...] = (out_ref[...] + tile(sequences - 1)) * (1.0 / sequences)
+        out_ref[...] += squares(index * group)
+
+    out_ref[...] = (out_ref[...] + squares(sequences - group)) * (1.0 / sequences)
 
 
 def fit(bounds, rot_grads, rot_inputs, sequences):
@@ -293,65 +301,66 @@
             up[k] = act_part[k]
 
         for half in range(2):
-            send_down(k, half, r == 0)
-            send_up(k, half, r == rows - 1)
-
-    def send_down(k, half, condition):
-        copy = remote(down.at[k, half], down.at[k, half], down_send.at[k, half],
+            pl.when(r == 0)(down_copy(k, half).start)
+            pl.when(r == rows - 1)(up_copy(k, half).start)
+
+    def down_copy(k, half):
+        return remote(down.at[k, half], down.at[k, half], down_send.at[k, half],
                       down_recv.at[k, half], (jnp.minimum(r + 1, rows - 1), c))
-        send(copy, condition)
-
-    def send_up(k, half, condition):
-        copy = remote(up.at[k, half], up.at[k, half], up_send.at[k, half],
+
+    def up_copy(k, half):
+        return remote(up.at[k, half], up.at[k, half], up_send.at[k, half],
                       up_recv.at[k, half], (jnp.maximum(r - 1, 0), c))
-        send(copy, condition)
+
+    def result_copy(k, half):
+        return pltpu.make_async_copy(
+            act_part.at[k, half], rot_inputs_ref.at[:, k, half], out_sem.at[rows + 2 * k + half]
+        )
+
+    def chain_step(flow, other, copy, index, has_next, is_second):
+        k, half = (chip + index // 2) % chips, index % 2
+        copy(k, half).wait_recv()
+
+        @pl.when(is_second)
+        def _():
+            @pl.loop(0, rows)
+            def _(q):
+                before = flow[k, half, q].astype(jnp.float32)
+                own = act_part[k, half, q].astype(jnp.float32)
+                rest = other[k, half, q].astype(jnp.float32)
+                flow[k, half, q] = (before + own).astype(jnp.bfloat16)
+                act_part[k, half, q] = (before + rest).astype(jnp.bfloat16)
+
+        @pl.when(jnp.logical_not(is_second))
+        def _():
+            @pl.loop(0, rows)
+            def _(q):
+                before = flow[k, half, q].astype(jnp.float32)
+                own = act_part[k, half, q].astype(jnp.float32)
+                flow[k, half, q] = (before + own).astype(jnp.bfloat16)
+
+        pl.when(has_next)(copy(k, half).start)
+        pl.when(is_second)(result_copy(k, half).start)
+
+    upper = 2 * r >= rows
+
+    def act_chain(time):
+        below, above = time - r, time - (rows - 1 - r)
+
+        @pl.when(jnp.logical_and(not_first, jnp.logical_and(below >= 0, below < cols)))
+        def _():
+            chain_step(down, up, down_copy, below, not_last, upper)
+
+        @pl.when(jnp.logical_and(not_last, jnp.logical_and(above >= 0, above < cols)))
+        def _():
+            chain_step(up, down, up_copy, above, not_first, jnp.logical_not(upper))
 
     stores = []
-
-    def act_chain(step):
-        k = (chip + step) % chips
-        for half in range(2):
-            @pl.when(not_first)
-            def _():
-                remote(down.at[k, half], down.at[k, half], down_send.at[k, half],
-                       down_recv.at[k, half], partner).wait_recv()
-
-                @pl.loop(0, rows)
-                def _(q):
-                    total = down[k, half, q].astype(jnp.float32)
-                    total = total + act_part[k, half, q].astype(jnp.float32)
-                    down[k, half, q] = total.astype(jnp.bfloat16)
-
-            send_down(k, half, jnp.logical_and(not_first, not_last))
-
-            @pl.when(not_last)
-            def _():
-                remote(up.at[k, half], up.at[k, half], up_send.at[k, half],
-                       up_recv.at[k, half], partner).wait_recv()
-
-                @pl.loop(0, rows)
-                def _(q):
-                    above = up[k, half, q].astype(jnp.float32)
-                    own = act_part[k, half, q].astype(jnp.float32)
-                    below = down[k, half, q].astype(jnp.float32)
-                    up[k, half, q] = (above + own).astype(jnp.bfloat16)
-                    act_part[k, half, q] = (above + below).astype(jnp.bfloat16)
-
-            @pl.when(r == rows - 1)
-            def _():
-                act_part[k, half] = down[k, half]
-
-            send_up(k, half, jnp.logical_and(not_first, not_last))
-            store = pltpu.make_async_copy(
-                act_part.at[k, half], rot_inputs_ref.at[:, k, half], out_sem.at[rows + 2 * step + half]
-            )
-            store.start()
-            stores.append(store)
-
     ticks = [functools.partial(grad_tick, t) for t in range(rows + 3)]
     rotates = [functools.partial(act_rotate, s) for s in range(chips)]
-    chains = [functools.partial(act_chain, s) for s in range(chips)]
-    for step in merged(ticks[: rows - 1], rotates) + merged(chains, ticks[rows - 1 :]):
+    chains = [functools.partial(act_chain, t) for t in range(1, cols + rows - 1)]
+    early = rows // 2
+    for step in merged(ticks[:early], rotates[:-1]) + rotates[-1:] + merged(chains, ticks[early:]):
         step()
     for slot in range(rows):
         block = blocks[slot]
@@ -364,6 +373,11 @@
             copy.wait_send()
         else:
             pl.when(condition)(copy.wait_send)
+    for k in range(chips):
+        for half in range(2):
+            pl.when(not_last)(down_copy(k, half).wait_send)
+            pl.when(not_first)(up_copy(k, half).wait_send)
+            result_copy(k, half).wait()
     for store in stores:
         store.wait()
 

time: 214 us -> 165 us (0.77)
  Pallas kernels: 197 us -> 147 us
    pallas_call x1, Pallas kernels: 172 us -> 133 us  [rotate(): pl.pallas_call(functools.partial(rotate_kernel, rows, cols), out_shape=(j...]
    pallas_call x1, Pallas kernels: 24.8 us -> 14.5 us  [fit(): pl.pallas_call(functools.partial(fit_kernel, sequences, window), grid=(ro...]
  transfers between devices with their start and end apart: 1 -> 1, of which waited for: 1 -> 1; matrix products, arithmetic and copies ran while one was open for 3% -> 4% of each run, Pallas kernels for 0% -> 0%
where the time goes in v2:
time: 165 us
  Pallas kernels  147 us (89%)
  local copies, waits for them, and re-layouts  5.43 us (3%)
  starting transfers between devices  4.5 us (3%)
  matrix products  3.48 us (2%)
  other arithmetic  3.11 us (2%)
    pallas_call x1, Pallas kernels, rotate(): pl.pallas_call(functools.partial(rotate_kernel, rows, cols), out_shape=(j...  133 us
    pallas_call x1, Pallas kernels, fit(): pl.pallas_call(functools.partial(fit_kernel, sequences, window), grid=(ro...  14.5 us
    ppermute x1, starting transfers between devices, from_behind(): lax.ppermute(value, axis, [(source, source + steps) for source in range(i...  4.5 us
    unnamed x4, local copies, waits for them, and re-layouts  3.77 us
  transfers between devices with their start and end apart: 1, of which 1 were waited for; matrix products, arithmetic and copies ran while one was open for 4% of the time, Pallas kernels for 0%

profile of v2, /device:TPU:1, one launch (start us, length us, event | category | flops | bytes accessed | tf_op | source)
XLA Modules:
  0.0 164.7 jit_solution(4182909793333456528)
XLA Ops:
  0.0 4.5 %collective-permute-start = (bf16[32,8192]{1,0:T(8,128)(2,1)}, bf16[32,8192]{1,0:T(8,128)(2,1)S(1)}, u32[]{:S(2)}, u32[]{:S(2)}) collective-permute-start(bf16[32,8192]{1,0:T(8,128)(2,1)} %param.8), channel_id=1, source_target_pairs={{0,1},{1,2},{2,3},{3,4},{4,5},{5,6},{6,7},{7,8},{8,9},{9,10},{10,1... | collective-permute-start | bytes 1572872 | tf_op jit(solution)/shard_map/ppermute | solution.py:17
  4.5 0.8 convert_reduce_fusion.1.bounds_ref
  5.3 0.8 dynamic_slice.3
  6.1 0.9 convert_reduce_fusion
  7.0 0.1 fusion.7
  7.0 1.3 multiply_reduce_fusion
  8.3 0.1 iota_subtract_fusion
  8.4 1.9 %convolution_convert_fusion.1 = bf16[32,64,64]{2,1,0:T(8,128)(2,1)S(1)} fusion(f32[32,64,32]{1,2,0:T(8,128)} %param.7, s32[32,32]{1,0:T(8,128)S(1)} %iota_subtract_fusion, f32[32,64]{1,0:T(8,128)S(1)} %multiply_reduce_fusion, f32[32,32]{1,0:T(8,128)S(1)} %fusion.7), kind=kOutput, calls=%fused_computation.1 | convolution fusion | flops 8781824 | bytes 540672 | tf_op jit(solution)/shard_map/phj,pjk->phk/dot_general | solution.py:98
  10.3 0.6 collective-permute-done
  10.9 1.6 fusion
  12.5 0.9 copy.22
  13.4 132.9 %shard_map.64 = (bf16[4,4,2,32,2048]{4,3,2,1,0:T(8,128)(2,1)}, bf16[4,4,2,32,1024]{4,3,2,1,0:T(8,128)(2,1)}) custom-call(bf16[32,8192]{1,0:T(8,128)(2,1)} %bitcast.17, bf16[32,8192]{1,0:T(8,128)(2,1)} %grads_ref.1, bf16[2048,1024]{1,0:T(8,128)(2,1)} %act_hbm.1, bf16[1024,2048]{1,0:T(8,128)(2,1)} %grad_hbm.1), custom_call_target="tpu_custom_call" | custom-call | flops 8589934592 | bytes 16777216 | tf_op jit(solution)/shard_map/pallas_call | solution.py:394
  146.4 0.0 copy-start
  146.4 2.2 %copy-done = bf16[4,4,2,32,2048]{4,3,2,1,0:T(8,128)(2,1)S(1)} copy-done((bf16[4,4,2,32,2048]{4,3,2,1,0:T(8,128)(2,1)S(1)}, bf16[4,4,2,32,2048]{4,3,2,1,0:T(8,128)(2,1)}, u32[]{:S(2)}) %copy-start) | copy-done | bytes 4194328
  148.6 0.0 copy-start.1
  148.6 1.6 copy-done.1
  150.2 14.5 %shard_map.65 = f32[2048,1024]{1,0:T(8,128)} custom-call(s32[9]{0:T(128)S(1)} %convert_reduce_fusion.1.bounds_ref, bf16[1024,2048]{1,0:T(8,128)(2,1)S(1)} %bitcast.15, bf16[1024,1024]{1,0:T(8,128)(2,1)S(1)} %bitcast.16), custom_call_target="tpu_custom_call" | custom-call | flops 8589934592 | bytes 14680064 | tf_op jit(solution)/shard_map/pallas_call | solution.py:59
  (2 shorter events, 0.0 us)
Async XLA Ops:
  0.0 10.9 %collective-permute-start = (bf16[32,8192]{1,0:T(8,128)(2,1)}, bf16[32,8192]{1,0:T(8,128)(2,1)S(1)}, u32[]{:S(2)}, u32[]{:S(2)}) collective-permute-start(bf16[32,8192]{1,0:T(8,128)(2,1)} %param.8), channel_id=1, source_target_pairs={{0,1},{1,2},{2,3},{3,4},{4,5},{5,6},{6,7},{7,8},{8,9},{9,10},{10,1... | collective-permute-start | bytes 1572872 | tf_op jit(solution)/shard_map/ppermute | solution.py:17
  146.4 2.2 %copy-start = (bf16[4,4,2,32,2048]{4,3,2,1,0:T(8,128)(2,1)S(1)}, bf16[4,4,2,32,2048]{4,3,2,1,0:T(8,128)(2,1)}, u32[]{:S(2)}) copy-start(bf16[4,4,2,32,2048]{4,3,2,1,0:T(8,128)(2,1)} %get-tuple-element.7) | copy-start | bytes 12582916
  148.6 1.6 copy-start.1

commit v3 on v2

--- a/solution.py
+++ b/solution.py
@@ -66,7 +66,7 @@
             pl.BlockSpec((total_tok, columns), lambda i: (0, 0)),
         ],
         out_specs=pl.BlockSpec((height, columns), lambda i: (i, 0)),
-        compiler_params=pltpu.CompilerParams(vmem_limit_bytes=32 * MIB),
+        compiler_params=pltpu.CompilerParams(vmem_limit_bytes=58 * MIB),
         cost_estimate=pl.CostEstimate(
             flops=2 * rows * columns * window * sequences,
             bytes_accessed=4 * rows * columns + 2 * total_tok * (rows + columns),
@@ -300,31 +300,41 @@
         def _():
             up[k] = act_part[k]
 
-        for half in range(2):
-            pl.when(r == 0)(down_copy(k, half).start)
-            pl.when(r == rows - 1)(up_copy(k, half).start)
-
-    def down_copy(k, half):
-        return remote(down.at[k, half], down.at[k, half], down_send.at[k, half],
-                      down_recv.at[k, half], (jnp.minimum(r + 1, rows - 1), c))
-
-    def up_copy(k, half):
-        return remote(up.at[k, half], up.at[k, half], up_send.at[k, half],
-                      up_recv.at[k, half], (jnp.maximum(r - 1, 0), c))
-
-    def result_copy(k, half):
+        for index in range(2 * pieces):
+            pl.when(r == 0)(down_copy(k, index).start)
+            pl.when(r == rows - 1)(up_copy(k, index).start)
+
+    pieces = 2
+    span = rows // pieces
+
+    def piece(ref, k, index):
+        return ref.at[k, index // pieces, pl.ds(index % pieces * span, span)]
+
+    def down_copy(k, index):
+        return remote(piece(down, k, index), piece(down, k, index), down_send.at[k, index],
+                      down_recv.at[k, index], (jnp.minimum(r + 1, rows - 1), c))
+
+    def up_copy(k, index):
+        return remote(piece(up, k, index), piece(up, k, index), up_send.at[k, index],
+                      up_recv.at[k, index], (jnp.maximum(r - 1, 0), c))
+
+    def result_copy(k, index):
         return pltpu.make_async_copy(
-            act_part.at[k, half], rot_inputs_ref.at[:, k, half], out_sem.at[rows + 2 * k + half]
+            piece(act_part, k, index),
+            rot_inputs_ref.at[pl.ds(index % pieces * span, span), k, index // pieces],
+            out_sem.at[rows + 2 * pieces * k + index],
         )
 
-    def chain_step(flow, other, copy, index, has_next, is_second):
-        k, half = (chip + index // 2) % chips, index % 2
-        copy(k, half).wait_recv()
+    def chain_step(flow, other, copy, number, has_next, is_second):
+        k, index = (chip + number // (2 * pieces)) % chips, number % (2 * pieces)
+        half, first = index // pieces, index % pieces * span
+        copy(k, index).wait_recv()
 
         @pl.when(is_second)
         def _():
-            @pl.loop(0, rows)
-            def _(q):
+            @pl.loop(0, span)
+            def _(step):
+                q = first + step
                 before = flow[k, half, q].astype(jnp.float32)
                 own = act_part[k, half, q].astype(jnp.float32)
                 rest = other[k, half, q].astype(jnp.float32)
@@ -333,32 +343,33 @@
 
         @pl.when(jnp.logical_not(is_second))
         def _():
-            @pl.loop(0, rows)
-            def _(q):
+            @pl.loop(0, span)
+            def _(step):
+                q = first + step
                 before = flow[k, half, q].astype(jnp.float32)
                 own = act_part[k, half, q].astype(jnp.float32)
                 flow[k, half, q] = (before + own).astype(jnp.bfloat16)
 
-        pl.when(has_next)(copy(k, half).start)
-        pl.when(is_second)(result_copy(k, half).start)
+        pl.when(has_next)(copy(k, index).start)
+        pl.when(is_second)(result_copy(k, index).start)
 
     upper = 2 * r >= rows
 
     def act_chain(time):
         below, above = time - r, time - (rows - 1 - r)
 
-        @pl.when(jnp.logical_and(not_first, jnp.logical_and(below >= 0, below < cols)))
+        @pl.when(jnp.logical_and(not_first, jnp.logical_and(below >= 0, below < cols * pieces)))
         def _():
             chain_step(down, up, down_copy, below, not_last, upper)
 
-        @pl.when(jnp.logical_and(not_last, jnp.logical_and(above >= 0, above < cols)))
+        @pl.when(jnp.logical_and(not_last, jnp.logical_and(above >= 0, above < cols * pieces)))
         def _():
             chain_step(up, down, up_copy, above, not_first, jnp.logical_not(upper))
 
     stores = []
     ticks = [functools.partial(grad_tick, t) for t in range(rows + 3)]
     rotates = [functools.partial(act_rotate, s) for s in range(chips)]
-    chains = [functools.partial(act_chain, t) for t in range(1, cols + rows - 1)]
+    chains = [functools.partial(act_chain, t) for t in range(1, cols * pieces + rows - 1)]
     early = rows // 2
     for step in merged(ticks[:early], rotates[:-1]) + rotates[-1:] + merged(chains, ticks[early:]):
         step()
@@ -374,10 +385,10 @@
         else:
             pl.when(condition)(copy.wait_send)
     for k in range(chips):
-        for half in range(2):
-            pl.when(not_last)(down_copy(k, half).wait_send)
-            pl.when(not_first)(up_copy(k, half).wait_send)
-            result_copy(k, half).wait()
+        for index in range(2 * pieces):
+            pl.when(not_last)(down_copy(k, index).wait_send)
+            pl.when(not_first)(up_copy(k, index).wait_send)
+            result_copy(k, index).wait()
     for store in stores:
         store.wait()
 
@@ -416,14 +427,14 @@
             vmem((chips, 2, rows, tok, act_width), bf16),
             vmem((chips, 2, rows, tok, act_width), bf16),
             vmem((chips, 2, rows, tok, act_width), bf16),
-            dma((2,)), dma((rows + cols,)),
+            dma((2,)), dma((rows + 2 * cols,)),
             dma((rows,)), dma((rows,)), dma((cols,)), dma((cols,)),
             dma((chips,)), dma((chips,)), dma((chips,)), dma((chips,)),
             dma((rows,)), dma((rows,)), dma((rows,)),
             dma((rows,)), dma((rows,)),
             dma((rows, chips)), dma((rows, chips)), dma((rows, chips)), dma((rows, chips)),
             dma((rows,)), dma((rows,)),
-            dma((chips, 2)), dma((chips, 2)), dma((chips, 2)), dma((chips, 2)),
+            dma((chips, 4)), dma((chips, 4)), dma((chips, 4)), dma((chips, 4)),
         ],
         compiler_params=pltpu.CompilerParams(
             collective_id=0, has_side_effects=True, vmem_limit_bytes=58 * MIB

time: 165 us -> 166 us (level)
  Pallas kernels: 147 us -> 152 us
  local copies, waits for them, and re-layouts: 5.43 us -> 1.66 us
    pallas_call x1, Pallas kernels: 133 us -> 137 us  [rotate(): pl.pallas_call(functools.partial(rotate_kernel, rows, cols), out_shape=(j...]
    unnamed x4 -> x0, local copies, waits for them, and re-layouts: 3.77 us -> none
where the time goes in v3:
time: 166 us
  Pallas kernels  152 us (92%)
  starting transfers between devices  4.5 us (3%)
  other arithmetic  3.62 us (2%)
  matrix products  3.46 us (2%)
    pallas_call x1, Pallas kernels, rotate(): pl.pallas_call(functools.partial(rotate_kernel, rows, cols), out_shape=(j...  137 us
    pallas_call x1, Pallas kernels, fit(): pl.pallas_call(functools.partial(fit_kernel, sequences, window), grid=(ro...  15.3 us
    ppermute x1, starting transfers between devices, from_behind(): lax.ppermute(value, axis, [(source, source + steps) for source in range(i...  4.5 us
  transfers between devices with their start and end apart: 1, of which 1 were waited for; matrix products, arithmetic and copies ran while one was open for 4% of the time, Pallas kernels for 0%

profile of v3, /device:TPU:1, one launch (start us, length us, event | category | flops | bytes accessed | tf_op | source)
XLA Modules:
  0.0 165.6 jit_solution(8202248540108590178)
XLA Ops:
  0.0 4.5 %collective-permute-start = (bf16[32,8192]{1,0:T(8,128)(2,1)}, bf16[32,8192]{1,0:T(8,128)(2,1)S(1)}, u32[]{:S(2)}, u32[]{:S(2)}) collective-permute-start(bf16[32,8192]{1,0:T(8,128)(2,1)} %param.8), channel_id=1, source_target_pairs={{0,1},{1,2},{2,3},{3,4},{4,5},{5,6},{6,7},{7,8},{8,9},{9,10},{10,1... | collective-permute-start | bytes 1572872 | tf_op jit(solution)/shard_map/ppermute | solution.py:17
  4.5 1.3 convert_reduce_fusion.1.bounds_ref
  5.8 0.8 dynamic_slice.3
  6.6 0.9 convert_reduce_fusion
  7.5 0.1 fusion.7
  7.6 1.3 multiply_reduce_fusion
  8.8 0.1 iota_subtract_fusion
  8.9 1.9 %convolution_convert_fusion.1 = bf16[32,64,64]{2,1,0:T(8,128)(2,1)S(1)} fusion(f32[32,64,32]{1,2,0:T(8,128)} %param.7, s32[32,32]{1,0:T(8,128)S(1)} %iota_subtract_fusion, f32[32,64]{1,0:T(8,128)S(1)} %multiply_reduce_fusion, f32[32,32]{1,0:T(8,128)S(1)} %fusion.7), kind=kOutput, calls=%fused_computation.1 | convolution fusion | flops 8781824 | bytes 540672 | tf_op jit(solution)/shard_map/phj,pjk->phk/dot_general | solution.py:98
  10.8 0.1 collective-permute-done
  10.9 1.6 fusion
  12.5 0.9 copy.22
  13.4 136.9 %shard_map.64 = (bf16[4,4,2,32,2048]{4,3,2,1,0:T(8,128)(2,1)}, bf16[4,4,2,32,1024]{4,3,2,1,0:T(8,128)(2,1)}) custom-call(bf16[32,8192]{1,0:T(8,128)(2,1)} %bitcast.15, bf16[32,8192]{1,0:T(8,128)(2,1)} %grads_ref.1, bf16[2048,1024]{1,0:T(8,128)(2,1)} %act_hbm.1, bf16[1024,2048]{1,0:T(8,128)(2,1)} %grad_hbm.1), custom_call_target="tpu_custom_call" | custom-call | flops 8589934592 | bytes 16777216 | tf_op jit(solution)/shard_map/pallas_call | solution.py:405
  150.4 15.3 %shard_map.65 = f32[2048,1024]{1,0:T(8,128)} custom-call(s32[9]{0:T(128)} %convert_reduce_fusion.1.bounds_ref, bf16[1024,2048]{1,0:T(8,128)(2,1)} %bitcast.16, bf16[1024,1024]{1,0:T(8,128)(2,1)} %bitcast.17), custom_call_target="tpu_custom_call" | custom-call | flops 8589934592 | bytes 14680064 | tf_op jit(solution)/shard_map/pallas_call | solution.py:59
  (2 shorter events, 0.0 us)
Async XLA Ops:
  0.0 10.9 %collective-permute-start = (bf16[32,8192]{1,0:T(8,128)(2,1)}, bf16[32,8192]{1,0:T(8,128)(2,1)S(1)}, u32[]{:S(2)}, u32[]{:S(2)}) collective-permute-start(bf16[32,8192]{1,0:T(8,128)(2,1)} %param.8), channel_id=1, source_target_pairs={{0,1},{1,2},{2,3},{3,4},{4,5},{5,6},{6,7},{7,8},{8,9},{9,10},{10,1... | collective-permute-start | bytes 1572872 | tf_op jit(solution)/shard_map/ppermute | solution.py:17

commit v4 on v2

--- a/solution.py
+++ b/solution.py
@@ -66,7 +66,7 @@
             pl.BlockSpec((total_tok, columns), lambda i: (0, 0)),
         ],
         out_specs=pl.BlockSpec((height, columns), lambda i: (i, 0)),
-        compiler_params=pltpu.CompilerParams(vmem_limit_bytes=32 * MIB),
+        compiler_params=pltpu.CompilerParams(vmem_limit_bytes=58 * MIB),
         cost_estimate=pl.CostEstimate(
             flops=2 * rows * columns * window * sequences,
             bytes_accessed=4 * rows * columns + 2 * total_tok * (rows + columns),

time: 165 us -> 162 us (0.982)
  local copies, waits for them, and re-layouts: 5.43 us -> 1.66 us
    unnamed x4 -> x0, local copies, waits for them, and re-layouts: 3.77 us -> none
where the time goes in v4:
time: 162 us
  Pallas kernels  148 us (91%)
  starting transfers between devices  4.5 us (3%)
  other arithmetic  3.62 us (2%)
  matrix products  3.46 us (2%)
  local copies, waits for them, and re-layouts  1.66 us (1%)
    pallas_call x1, Pallas kernels, rotate(): pl.pallas_call(functools.partial(rotate_kernel, rows, cols), out_shape=(j...  133 us
    pallas_call x1, Pallas kernels, fit(): pl.pallas_call(functools.partial(fit_kernel, sequences, window), grid=(ro...  15.4 us
    ppermute x1, starting transfers between devices, from_behind(): lax.ppermute(value, axis, [(source, source + steps) for source in range(i...  4.5 us
  transfers between devices with their start and end apart: 1, of which 1 were waited for; matrix products, arithmetic and copies ran while one was open for 4% of the time, Pallas kernels for 0%

profile of v4, /device:TPU:1, one launch (start us, length us, event | category | flops | bytes accessed | tf_op | source)
XLA Modules:
  0.0 161.8 jit_solution(9884578403960651345)
XLA Ops:
  0.0 4.5 %collective-permute-start = (bf16[32,8192]{1,0:T(8,128)(2,1)}, bf16[32,8192]{1,0:T(8,128)(2,1)S(1)}, u32[]{:S(2)}, u32[]{:S(2)}) collective-permute-start(bf16[32,8192]{1,0:T(8,128)(2,1)} %param.8), channel_id=1, source_target_pairs={{0,1},{1,2},{2,3},{3,4},{4,5},{5,6},{6,7},{7,8},{8,9},{9,10},{10,1... | collective-permute-start | bytes 1572872 | tf_op jit(solution)/shard_map/ppermute | solution.py:17
  4.5 1.3 convert_reduce_fusion.1.bounds_ref
  5.8 0.8 dynamic_slice.3
  6.6 0.9 convert_reduce_fusion
  7.5 0.1 fusion.7
  7.6 1.3 multiply_reduce_fusion
  8.8 0.1 iota_subtract_fusion
  8.9 1.9 %convolution_convert_fusion.1 = bf16[32,64,64]{2,1,0:T(8,128)(2,1)S(1)} fusion(f32[32,64,32]{1,2,0:T(8,128)} %param.7, s32[32,32]{1,0:T(8,128)S(1)} %iota_subtract_fusion, f32[32,64]{1,0:T(8,128)S(1)} %multiply_reduce_fusion, f32[32,32]{1,0:T(8,128)S(1)} %fusion.7), kind=kOutput, calls=%fused_computation.1 | convolution fusion | flops 8781824 | bytes 540672 | tf_op jit(solution)/shard_map/phj,pjk->phk/dot_general | solution.py:98
  10.8 0.1 collective-permute-done
  10.9 1.6 fusion
  12.5 0.9 copy.22
  13.4 132.9 %shard_map.64 = (bf16[4,4,2,32,2048]{4,3,2,1,0:T(8,128)(2,1)}, bf16[4,4,2,32,1024]{4,3,2,1,0:T(8,128)(2,1)}) custom-call(bf16[32,8192]{1,0:T(8,128)(2,1)} %bitcast.15, bf16[32,8192]{1,0:T(8,128)(2,1)} %grads_ref.1, bf16[2048,1024]{1,0:T(8,128)(2,1)} %act_hbm.1, bf16[1024,2048]{1,0:T(8,128)(2,1)} %grad_hbm.1), custom_call_target="tpu_custom_call" | custom-call | flops 8589934592 | bytes 16777216 | tf_op jit(solution)/shard_map/pallas_call | solution.py:394
  146.4 15.4 %shard_map.65 = f32[2048,1024]{1,0:T(8,128)} custom-call(s32[9]{0:T(128)} %convert_reduce_fusion.1.bounds_ref, bf16[1024,2048]{1,0:T(8,128)(2,1)} %bitcast.16, bf16[1024,1024]{1,0:T(8,128)(2,1)} %bitcast.17), custom_call_target="tpu_custom_call" | custom-call | flops 8589934592 | bytes 14680064 | tf_op jit(solution)/shard_map/pallas_call | solution.py:59
  (2 shorter events, 0.0 us)
Async XLA Ops:
  0.0 10.9 %collective-permute-start = (bf16[32,8192]{1,0:T(8,128)(2,1)}, bf16[32,8192]{1,0:T(8,128)(2,1)S(1)}, u32[]{:S(2)}, u32[]{:S(2)}) collective-permute-start(bf16[32,8192]{1,0:T(8,128)(2,1)} %param.8), channel_id=1, source_target_pairs={{0,1},{1,2},{2,3},{3,4},{4,5},{5,6},{6,7},{7,8},{8,9},{9,10},{10,1... | collective-permute-start | bytes 1572872 | tf_op jit(solution)/shard_map/ppermute | solution.py:17
